TPU v7x, 32 devices: a whole 2x2x4 slice. The times are simulated.
32 devices in a mesh: row: 4 (over z), col: 8 (over y, x, core).
Axes of the slice: x: 2, y: 2, z: 4, core: 2. Of those that a mesh axis runs over, the one named last changes fastest.
Arguments:
- source_tiles: bfloat16 [4, 8, 1024, 128], P('row', 'col'), may hold values from -6 to 6
- requests: int32 [4, 8, 8, 256], P('row', 'col'), may hold values from 0 to 1023
- stencil: int32 [128, 256, 4], P('row', 'col'), may hold values from 0 to 2047, as said below
- regrid_weight: float32 [128, 256, 4], P('row', 'col'), may hold values from 0.1 to 0.6
- w_in: bfloat16 [3, 3, 64, 128], replicated, may hold values from -0.4375 to 0.4375
- w_enc: bfloat16 [3, 3, 128, 128], replicated, may hold values from -0.3125 to 0.3125
- w_mid_first: bfloat16 [3, 3, 128, 128], replicated, may hold values from -0.3125 to 0.3125
- w_mid_second: bfloat16 [3, 3, 128, 128], replicated, may hold values from -0.3125 to 0.3125
- w_dec_first: bfloat16 [3, 3, 256, 128], replicated, may hold values from -0.21875 to 0.21875
- w_dec_second: bfloat16 [3, 3, 128, 128], replicated, may hold values from -0.3125 to 0.3125
- w_out: bfloat16 [128, 64], replicated, may hold values from -0.75 to 0.75
Outputs:
- forecast: bfloat16 [128, 256, 2, 64], P('row', 'col')
Inputs may be any that keep to these rules, and one draw needn't show every extreme that they name: `stencil`: within each device's 32 x 32 block of target cells, every slot 0 to 2047 appears at least once among the entries.
All inputs are finite; a program needn't handle non-finite values.
Results may differ from a plain program's by a relative error of at most 0.017.
Values may be sent and summed in bfloat16 or wider, within the bound.
A program may use at most 64 MiB of HBM per device.

v0:
```python
import jax
import jax.numpy as jnp
from jax import lax
from jax.sharding import PartitionSpec as P

FIELDS = 64
CH = 128


def with_halo(x, sides, width):
    for axis, dim in sides:
        devices, length = (lax.axis_size(axis), x.shape[dim])
        up = [(i, (i + 1) % devices) for i in range(devices)]
        down = [(j, i) for i, j in up]
        last = lax.slice_in_dim(x, length - width, length, axis=dim)
        leading = lax.slice_in_dim(x, 0, width, axis=dim)
        before = lax.ppermute(last, axis, up)
        after = lax.ppermute(leading, axis, down)
        x = jnp.concatenate([before, x, after], axis=dim)
    return x


def conv_valid(padded, weight):
    height = padded.shape[0] - 2
    width = padded.shape[1] - 2
    samples = padded.shape[2]
    inner = padded.shape[3]
    outer = weight.shape[3]
    total = jnp.zeros((height * width * samples, outer), jnp.float32)
    for row_step in range(3):
        for col_step in range(3):
            window = padded[row_step : row_step + height, col_step : col_step + width].reshape(
                -1, inner
            )
            total = total + jnp.dot(
                window, weight[row_step, col_step], preferred_element_type=jnp.float32
            )
    return jax.nn.silu(total).reshape(height, width, samples, outer).astype(jnp.bfloat16)


def rim_clear(padded, depth, rows_dev):
    global_rows = (
        lax.axis_index("row") * rows_dev + jnp.arange(padded.shape[0], dtype=jnp.int32) - depth
    )
    inside = (global_rows >= 0) & (global_rows < lax.axis_size("row") * rows_dev)
    return jnp.where(inside[:, None, None, None], padded, jnp.zeros_like(padded))


def body(
    source_tiles,
    requests,
    stencil,
    regrid_weight,
    w_in,
    w_enc,
    w_mid_first,
    w_mid_second,
    w_dec_first,
    w_dec_second,
    w_out,
):
    tile_rows = stencil.shape[0]
    tile_cols = stencil.shape[1]
    columns = source_tiles.shape[3]
    samples = columns // FIELDS
    cells = source_tiles.shape[2]
    groups = requests.shape[2]
    capacity = requests.shape[3]
    wanted = requests.reshape(groups, capacity)
    global_ids = (jnp.arange(groups, dtype=jnp.int32)[:, None] * cells + wanted).reshape(-1)
    empty = jnp.zeros((groups * capacity, columns), jnp.bfloat16)
    flattened = lax.all_gather(source_tiles, "col", axis=1, tiled=True).reshape(-1, columns)
    inside = (global_ids >= 0) & (global_ids < flattened.shape[0])
    picked = flattened[jnp.clip(global_ids, 0, flattened.shape[0] - 1)]
    buffer = jnp.where(inside[:, None], picked, empty)
    picked = buffer[stencil]
    regridded = jnp.sum(picked.astype(jnp.float32) * regrid_weight[..., None], axis=2).astype(
        jnp.bfloat16
    )
    regridded = regridded.reshape(tile_rows, tile_cols, samples, FIELDS)
    padded = rim_clear(with_halo(regridded, (("row", 0), ("col", 1)), 1), 1, tile_rows)
    first = conv_valid(padded, w_in)
    padded = rim_clear(with_halo(first, (("row", 0), ("col", 1)), 1), 1, tile_rows)
    skip = conv_valid(padded, w_enc)
    half_rows = tile_rows // 2
    half_cols = tile_cols // 2
    pooled = (
        skip.astype(jnp.float32)
        .reshape(half_rows, 2, half_cols, 2, samples, CH)
        .mean(axis=(1, 3))
        .astype(jnp.bfloat16)
    )
    padded = rim_clear(with_halo(pooled, (("row", 0), ("col", 1)), 1), 1, half_rows)
    middle = conv_valid(padded, w_mid_first)
    padded = rim_clear(with_halo(middle, (("row", 0), ("col", 1)), 1), 1, half_rows)
    coarse = conv_valid(padded, w_mid_second)
    upsampled = jnp.repeat(jnp.repeat(coarse, 2, axis=0), 2, axis=1)
    joined = jnp.concatenate([upsampled, skip], axis=-1)
    padded = rim_clear(with_halo(joined, (("row", 0), ("col", 1)), 1), 1, tile_rows)
    decoded_first = conv_valid(padded, w_dec_first)
    padded = rim_clear(with_halo(decoded_first, (("row", 0), ("col", 1)), 1), 1, tile_rows)
    decoded = conv_valid(padded, w_dec_second)
    result = jnp.dot(decoded.reshape(-1, CH), w_out, preferred_element_type=jnp.float32)
    return result.reshape(tile_rows, tile_cols, samples, FIELDS).astype(jnp.bfloat16)


def solution(mesh):
    placed = (
        P("row", "col", None, None),
        P("row", "col", None, None),
        P("row", "col", None),
        P("row", "col", None),
        P(),
        P(),
        P(),
        P(),
        P(),
        P(),
        P(),
    )
    return jax.shard_map(
        body, mesh=mesh, in_specs=placed, out_specs=P("row", "col", None, None), check_vma=False
    )
```

profile of v0, /device:TPU:3, one launch (start us, length us, event | category | flops | bytes accessed | tf_op | source)
XLA Modules:
  0.0 215.8 jit_solution(13235562589627824381)
XLA Ops:
  11.3 27.5 %all-gather.2.cloned.1.call-done = bf16[1,8,1024,128]{3,2,0,1:T(8,128)(2,1)} async-done(((bf16[1,1,1024,128]{3,2,0,1:T(8,128)(2,1)}), bf16[1,8,1024,128]{3,2,0,1:T(8,128)(2,1)}) %all-gather.2.cloned.1.call-update) | async-done | bytes 2097168 | tf_op jit(solution)/shard_map/all_gather | solution.py:72
  38.8 7.5 %gather_fusion = bf16[2048,128]{1,0:T(8,128)(2,1)S(1)} fusion(bf16[8192,128]{1,0:T(8,128)(2,1)} %bitcast.301, s32[2048]{0:T(1024)S(1)} %broadcast_clamp_fusion.1), kind=kCustom, calls=%fused_computation | custom fusion | bytes 1056768 | tf_op jit(solution)/shard_map/gather | solution.py:74
  46.6 12.1 %gather_fusion.1 = bf16[4096,128]{1,0:T(8,128)(2,1)S(1)} fusion(bf16[2048,128]{1,0:T(8,128)(2,1)S(1)} %broadcast_select_fusion.4, s32[4096]{0:T(1024)S(1)} %broadcast_clamp_fusion), kind=kCustom, calls=%fused_computation.1 | custom fusion | bytes 2113536 | tf_op jit(solution)/shard_map/gather | solution.py:76
  65.5 2.6 %collective-permute-start.2 = (bf16[34,1,2,64]{3,2,1,0:T(2,128)(2,1)S(1)}, bf16[34,1,2,64]{3,2,1,0:T(2,128)(2,1)S(1)}, u32[]{:S(2)}, u32[]{:S(2)}) collective-permute-start(bf16[34,1,2,64]{3,2,1,0:T(2,128)(2,1)S(1)} %get-tuple-element.49), channel_id=1, source_target_pairs={{0,1},{1,2},{2,3},{3,4},{4,5},{5,6},{6,7},{7,0},{8,9},{9,10},{10,1... | collective-permute-start | bytes 26120 | tf_op jit(solution)/shard_map/ppermute | solution.py:17
  69.0 3.2 %collective-permute-done.3 = bf16[34,1,2,64]{3,2,1,0:T(2,128)(2,1)S(1)} collective-permute-done((bf16[34,1,2,64]{3,2,1,0:T(2,128)(2,1)S(1)}, bf16[34,1,2,64]{3,2,1,0:T(2,128)(2,1)S(1)}, u32[]{:S(2)}, u32[]{:S(2)}) %collective-permute-start.3) | collective-permute-done | bytes 8736 | tf_op jit(solution)/shard_map/ppermute | solution.py:18
  73.3 5.2 %fusion.120 = (bf16[32,32,2,64]{3,2,1,0:T(2,128)(2,1)S(1)}, bf16[32,32,2,64]{3,2,1,0:T(2,128)(2,1)S(1)}, bf16[32,32,2,64]{3,2,1,0:T(2,128)(2,1)S(1)}, bf16[32,32...) fusion(bf16[34,34,2,64]{3,2,1,0:T(2,128)(2,1)S(1)} %broadcast_s, ...), kind=kLoop, calls=%fused_computation.218 | loop fusion | bytes 4718592 | tf_op jit(solution)/shard_map/slice | solution.py:32
  81.2 3.2 %collective-permute-start.5 = (bf16[1,32,2,128]{3,2,1,0:T(2,128)(2,1)S(1)}, bf16[1,32,2,128]{3,2,1,0:T(2,128)(2,1)S(1)}, u32[]{:S(2)}, u32[]{:S(2)}) collective-permute-start(bf16[1,32,2,128]{3,2,1,0:T(2,128)(2,1)S(1)} %bitcast.373), channel_id=1, source_target_pairs={{8,0},{16,8},{24,16},{0,24},{9,1},{17,9},{25,17},{1,25},{10,2},{18... | collective-permute-start | bytes 49160 | tf_op jit(solution)/shard_map/ppermute | solution.py:18
  85.3 3.5 %collective-permute-done.4 = bf16[1,32,2,128]{3,2,1,0:T(2,128)(2,1)S(1)} collective-permute-done((bf16[1,32,2,128]{3,2,1,0:T(2,128)(2,1)S(1)}, bf16[1,32,2,128]{3,2,1,0:T(2,128)(2,1)S(1)}, u32[]{:S(2)}, u32[]{:S(2)}) %collective-permute-start.4) | collective-permute-done | bytes 16416 | tf_op jit(solution)/shard_map/ppermute | solution.py:17
  91.2 3.2 %collective-permute-done.7 = bf16[34,1,2,128]{3,2,1,0:T(2,128)(2,1)S(1)} collective-permute-done((bf16[34,1,2,128]{3,2,1,0:T(2,128)(2,1)S(1)}, bf16[34,1,2,128]{3,2,1,0:T(2,128)(2,1)S(1)}, u32[]{:S(2)}, u32[]{:S(2)}) %collective-permute-start.7) | collective-permute-done | bytes 17440 | tf_op jit(solution)/shard_map/ppermute | solution.py:18
  96.2 5.2 %fusion.119 = (bf16[32,32,2,128]{3,2,1,0:T(2,128)(2,1)S(1)}, bf16[32,32,2,128]{3,2,1,0:T(2,128)(2,1)S(1)}, bf16[32,32,2,128]{3,2,1,0:T(2,128)(2,1)S(1)}, bf16[32...) fusion(bf16[34,34,2,128]{3,2,1,0:T(2,128)(2,1)S(1)} %broadcast_, ...), kind=kLoop, calls=%fused_computation.217 | loop fusion | bytes 9437184 | tf_op jit(solution)/shard_map/slice | solution.py:32
  104.9 3.3 %collective-permute-start.9 = (bf16[1,16,2,128]{3,2,1,0:T(2,128)(2,1)S(1)}, bf16[1,16,2,128]{3,2,1,0:T(2,128)(2,1)S(1)}, u32[]{:S(2)}, u32[]{:S(2)}) collective-permute-start(bf16[1,16,2,128]{3,2,1,0:T(2,128)(2,1)S(1)} %get-tuple-element.82), channel_id=1, source_target_pairs={{8,0},{16,8},{24,16},{0,24},{9,1},{17,9},{25,17},{1,25},{10,2},{18... | collective-permute-start | bytes 24584 | tf_op jit(solution)/shard_map/ppermute | solution.py:18
  111.4 3.2 %collective-permute-done.11 = bf16[18,1,2,128]{3,2,1,0:T(2,128)(2,1)S(1)} collective-permute-done((bf16[18,1,2,128]{3,2,1,0:T(2,128)(2,1)S(1)}, bf16[18,1,2,128]{3,2,1,0:T(2,128)(2,1)S(1)}, u32[]{:S(2)}, u32[]{:S(2)}) %collective-permute-start.11) | collective-permute-done | bytes 9248 | tf_op jit(solution)/shard_map/ppermute | solution.py:18
  117.3 3.6 %collective-permute-start.13 = (bf16[1,16,2,128]{3,2,1,0:T(2,128)(2,1)S(1)}, bf16[1,16,2,128]{3,2,1,0:T(2,128)(2,1)S(1)}, u32[]{:S(2)}, u32[]{:S(2)}) collective-permute-start(bf16[1,16,2,128]{3,2,1,0:T(2,128)(2,1)S(1)} %bitcast.376), channel_id=1, source_target_pairs={{8,0},{16,8},{24,16},{0,24},{9,1},{17,9},{25,17},{1,25},{10,2},{18... | collective-permute-start | bytes 24584 | tf_op jit(solution)/shard_map/ppermute | solution.py:18
  121.7 3.5 %collective-permute-done.12 = bf16[1,16,2,128]{3,2,1,0:T(2,128)(2,1)S(1)} collective-permute-done((bf16[1,16,2,128]{3,2,1,0:T(2,128)(2,1)S(1)}, bf16[1,16,2,128]{3,2,1,0:T(2,128)(2,1)S(1)}, u32[]{:S(2)}, u32[]{:S(2)}) %collective-permute-start.12) | collective-permute-done | bytes 8224 | tf_op jit(solution)/shard_map/ppermute | solution.py:17
  127.5 3.2 %collective-permute-done.15 = bf16[18,1,2,128]{3,2,1,0:T(2,128)(2,1)S(1)} collective-permute-done((bf16[18,1,2,128]{3,2,1,0:T(2,128)(2,1)S(1)}, bf16[18,1,2,128]{3,2,1,0:T(2,128)(2,1)S(1)}, u32[]{:S(2)}, u32[]{:S(2)}) %collective-permute-start.15) | collective-permute-done | bytes 9248 | tf_op jit(solution)/shard_map/ppermute | solution.py:18
  134.1 3.3 %collective-permute-start.17 = (bf16[1,32,2,256]{3,2,1,0:T(2,128)(2,1)S(1)}, bf16[1,32,2,256]{3,2,1,0:T(2,128)(2,1)S(1)}, u32[]{:S(2)}, u32[]{:S(2)}) collective-permute-start(bf16[1,32,2,256]{3,2,1,0:T(2,128)(2,1)S(1)} %get-tuple-element.17), channel_id=1, source_target_pairs={{8,0},{16,8},{24,16},{0,24},{9,1},{17,9},{25,17},{1,25},{10,2},{18... | collective-permute-start | bytes 98312 | tf_op jit(solution)/shard_map/ppermute | solution.py:18
  141.0 3.2 %collective-permute-done.19 = bf16[34,1,2,256]{3,2,1,0:T(2,128)(2,1)S(1)} collective-permute-done((bf16[34,1,2,256]{3,2,1,0:T(2,128)(2,1)S(1)}, bf16[34,1,2,256]{3,2,1,0:T(2,128)(2,1)S(1)}, u32[]{:S(2)}, u32[]{:S(2)}) %collective-permute-start.19) | collective-permute-done | bytes 34848 | tf_op jit(solution)/shard_map/ppermute | solution.py:18
  144.2 5.8 %broadcast_select_fusion = bf16[34,34,2,256]{3,2,1,0:T(2,128)(2,1)S(1)} fusion(pred[34]{0:T(512)(128)(4,1)S(1)} %compare_and_fusion.2, bf16[34,1,2,256]{3,2,1,0:T(2,128)(2,1)S(1)} %collective-permute-done.19, bf16[1,32,2,256]{3,2,1,0:T(2,128)(2,1)S(1)} %collective-permute-done.17, bf16[32,32,2,128]{3,2,1,0:T(2,128)(2,1)S(1)} %bitcast.305, ...), kind=kLoop, calls=%fused_computation.34 | loop fusion | flops 7694336 | bytes 2367522 | tf_op jit(solution)/shard_map/jit(_where)/select_n | solution.py:46
  150.0 10.8 %fusion.117 = (bf16[32,32,2,256]{3,2,1,0:T(2,128)(2,1)S(1)}, bf16[32,32,2,256]{3,2,1,0:T(2,128)(2,1)S(1)}, bf16[32,32,2,256]{3,2,1,0:T(2,128)(2,1)S(1)}, bf16[32...) fusion(bf16[34,34,2,256]{3,2,1,0:T(2,128)(2,1)S(1)} %broadcast_, ...), kind=kLoop, calls=%fused_computation.215 | loop fusion | bytes 18874368 | tf_op jit(solution)/shard_map/slice | solution.py:32
  166.5 2.3 %reshape.313 = bf16[2048,256]{1,0:T(8,128)(2,1)} reshape(bf16[32,32,2,256]{3,2,1,0:T(2,128)(2,1)} %get-tuple-element.10) | data formatting | bytes 2097152 | tf_op jit(solution)/shard_map/reshape | solution.py:32
  184.0 3.6 %collective-permute-start.21 = (bf16[1,32,2,128]{3,2,1,0:T(2,128)(2,1)S(1)}, bf16[1,32,2,128]{3,2,1,0:T(2,128)(2,1)S(1)}, u32[]{:S(2)}, u32[]{:S(2)}) collective-permute-start(bf16[1,32,2,128]{3,2,1,0:T(2,128)(2,1)S(1)} %bitcast.374), channel_id=1, source_target_pairs={{8,0},{16,8},{24,16},{0,24},{9,1},{17,9},{25,17},{1,25},{10,2},{18... | collective-permute-start | bytes 49160 | tf_op jit(solution)/shard_map/ppermute | solution.py:18
  188.5 3.5 %collective-permute-done.20 = bf16[1,32,2,128]{3,2,1,0:T(2,128)(2,1)S(1)} collective-permute-done((bf16[1,32,2,128]{3,2,1,0:T(2,128)(2,1)S(1)}, bf16[1,32,2,128]{3,2,1,0:T(2,128)(2,1)S(1)}, u32[]{:S(2)}, u32[]{:S(2)}) %collective-permute-start.20) | collective-permute-done | bytes 16416 | tf_op jit(solution)/shard_map/ppermute | solution.py:17
  194.4 3.2 %collective-permute-done.23 = bf16[34,1,2,128]{3,2,1,0:T(2,128)(2,1)S(1)} collective-permute-done((bf16[34,1,2,128]{3,2,1,0:T(2,128)(2,1)S(1)}, bf16[34,1,2,128]{3,2,1,0:T(2,128)(2,1)S(1)}, u32[]{:S(2)}, u32[]{:S(2)}) %collective-permute-start.23) | collective-permute-done | bytes 17440 | tf_op jit(solution)/shard_map/ppermute | solution.py:18
  199.4 5.2 %fusion.118 = (bf16[32,32,2,128]{3,2,1,0:T(2,128)(2,1)S(1)}, bf16[32,32,2,128]{3,2,1,0:T(2,128)(2,1)S(1)}, bf16[32,32,2,128]{3,2,1,0:T(2,128)(2,1)S(1)}, bf16[32...) fusion(bf16[34,34,2,128]{3,2,1,0:T(2,128)(2,1)S(1)} %broadcast_, ...), kind=kLoop, calls=%fused_computation.216 | loop fusion | bytes 9437184 | tf_op jit(solution)/shard_map/slice | solution.py:32
  (170 shorter events, 70.8 us)
Async XLA Ops:
  6.5 32.3 %all-gather.2.cloned.1.call-start = ((), (), s32[]{:S(2)}) async-start(), calls=%async_computation | async-start | bytes 2359296 | tf_op jit(solution)/shard_map/all_gather | solution.py:72
  60.5 4.4 %collective-permute-start = (bf16[1,32,2,64]{3,2,1,0:T(2,128)(2,1)S(1)}, bf16[1,32,2,64]{3,2,1,0:T(2,128)(2,1)S(1)}, u32[]{:S(2)}, u32[]{:S(2)}) collective-permute-start(bf16[1,32,2,64]{3,2,1,0:T(2,128)(2,1)S(1)} %slice.421), channel_id=1, source_target_pairs={{0,8},{8,16},{16,24},{24,0},{1,9},{9,17},{17,25},{25,1},{2,10},{10... | collective-permute-start | bytes 24584 | tf_op jit(solution)/shard_map/ppermute | solution.py:17
  62.0 3.4 %collective-permute-start.1 = (bf16[1,32,2,64]{3,2,1,0:T(2,128)(2,1)S(1)}, bf16[1,32,2,64]{3,2,1,0:T(2,128)(2,1)S(1)}, u32[]{:S(2)}, u32[]{:S(2)}) collective-permute-start(bf16[1,32,2,64]{3,2,1,0:T(2,128)(2,1)S(1)} %slice.423), channel_id=1, source_target_pairs={{8,0},{16,8},{24,16},{0,24},{9,1},{17,9},{25,17},{1,25},{10,2},{18... | collective-permute-start | bytes 24584 | tf_op jit(solution)/shard_map/ppermute | solution.py:18
  65.5 3.5 %collective-permute-start.2 = (bf16[34,1,2,64]{3,2,1,0:T(2,128)(2,1)S(1)}, bf16[34,1,2,64]{3,2,1,0:T(2,128)(2,1)S(1)}, u32[]{:S(2)}, u32[]{:S(2)}) collective-permute-start(bf16[34,1,2,64]{3,2,1,0:T(2,128)(2,1)S(1)} %get-tuple-element.49), channel_id=1, source_target_pairs={{0,1},{1,2},{2,3},{3,4},{4,5},{5,6},{6,7},{7,0},{8,9},{9,10},{10,1... | collective-permute-start | bytes 26120 | tf_op jit(solution)/shard_map/ppermute | solution.py:17
  68.1 4.1 %collective-permute-start.3 = (bf16[34,1,2,64]{3,2,1,0:T(2,128)(2,1)S(1)}, bf16[34,1,2,64]{3,2,1,0:T(2,128)(2,1)S(1)}, u32[]{:S(2)}, u32[]{:S(2)}) collective-permute-start(bf16[34,1,2,64]{3,2,1,0:T(2,128)(2,1)S(1)} %get-tuple-element.50), channel_id=1, source_target_pairs={{1,0},{2,1},{3,2},{4,3},{5,4},{6,5},{7,6},{0,7},{9,8},{10,9},{11,1... | collective-permute-start | bytes 26120 | tf_op jit(solution)/shard_map/ppermute | solution.py:18
  81.2 4.0 %collective-permute-start.5 = (bf16[1,32,2,128]{3,2,1,0:T(2,128)(2,1)S(1)}, bf16[1,32,2,128]{3,2,1,0:T(2,128)(2,1)S(1)}, u32[]{:S(2)}, u32[]{:S(2)}) collective-permute-start(bf16[1,32,2,128]{3,2,1,0:T(2,128)(2,1)S(1)} %bitcast.373), channel_id=1, source_target_pairs={{8,0},{16,8},{24,16},{0,24},{9,1},{17,9},{25,17},{1,25},{10,2},{18... | collective-permute-start | bytes 49160 | tf_op jit(solution)/shard_map/ppermute | solution.py:18
  84.4 4.4 %collective-permute-start.4 = (bf16[1,32,2,128]{3,2,1,0:T(2,128)(2,1)S(1)}, bf16[1,32,2,128]{3,2,1,0:T(2,128)(2,1)S(1)}, u32[]{:S(2)}, u32[]{:S(2)}) collective-permute-start(bf16[1,32,2,128]{3,2,1,0:T(2,128)(2,1)S(1)} %bitcast.371), channel_id=1, source_target_pairs={{0,8},{8,16},{16,24},{24,0},{1,9},{9,17},{17,25},{25,1},{2,10},{10... | collective-permute-start | bytes 49160 | tf_op jit(solution)/shard_map/ppermute | solution.py:17
  88.8 2.4 %collective-permute-start.6 = (bf16[34,1,2,128]{3,2,1,0:T(2,128)(2,1)S(1)}, bf16[34,1,2,128]{3,2,1,0:T(2,128)(2,1)S(1)}, u32[]{:S(2)}, u32[]{:S(2)}) collective-permute-start(bf16[34,1,2,128]{3,2,1,0:T(2,128)(2,1)S(1)} %get-tuple-element.47), channel_id=1, source_target_pairs={{0,1},{1,2},{2,3},{3,4},{4,5},{5,6},{6,7},{7,0},{8,9},{9,10},{10,1... | collective-permute-start | bytes 52232 | tf_op jit(solution)/shard_map/ppermute | solution.py:17
  90.4 4.1 %collective-permute-start.7 = (bf16[34,1,2,128]{3,2,1,0:T(2,128)(2,1)S(1)}, bf16[34,1,2,128]{3,2,1,0:T(2,128)(2,1)S(1)}, u32[]{:S(2)}, u32[]{:S(2)}) collective-permute-start(bf16[34,1,2,128]{3,2,1,0:T(2,128)(2,1)S(1)} %get-tuple-element.48), channel_id=1, source_target_pairs={{1,0},{2,1},{3,2},{4,3},{5,4},{6,5},{7,6},{0,7},{9,8},{10,9},{11,1... | collective-permute-start | bytes 52232 | tf_op jit(solution)/shard_map/ppermute | solution.py:18
  104.9 4.4 %collective-permute-start.8 = (bf16[1,16,2,128]{3,2,1,0:T(2,128)(2,1)S(1)}, bf16[1,16,2,128]{3,2,1,0:T(2,128)(2,1)S(1)}, u32[]{:S(2)}, u32[]{:S(2)}) collective-permute-start(bf16[1,16,2,128]{3,2,1,0:T(2,128)(2,1)S(1)} %get-tuple-element.81), channel_id=1, source_target_pairs={{0,8},{8,16},{16,24},{24,0},{1,9},{9,17},{17,25},{25,1},{2,10},{10... | collective-permute-start | bytes 24584 | tf_op jit(solution)/shard_map/ppermute | solution.py:17
  104.9 4.3 %collective-permute-start.9 = (bf16[1,16,2,128]{3,2,1,0:T(2,128)(2,1)S(1)}, bf16[1,16,2,128]{3,2,1,0:T(2,128)(2,1)S(1)}, u32[]{:S(2)}, u32[]{:S(2)}) collective-permute-start(bf16[1,16,2,128]{3,2,1,0:T(2,128)(2,1)S(1)} %get-tuple-element.82), channel_id=1, source_target_pairs={{8,0},{16,8},{24,16},{0,24},{9,1},{17,9},{25,17},{1,25},{10,2},{18... | collective-permute-start | bytes 24584 | tf_op jit(solution)/shard_map/ppermute | solution.py:18
  110.6 4.0 %collective-permute-start.11 = (bf16[18,1,2,128]{3,2,1,0:T(2,128)(2,1)S(1)}, bf16[18,1,2,128]{3,2,1,0:T(2,128)(2,1)S(1)}, u32[]{:S(2)}, u32[]{:S(2)}) collective-permute-start(bf16[18,1,2,128]{3,2,1,0:T(2,128)(2,1)S(1)} %get-tuple-element.78), channel_id=1, source_target_pairs={{1,0},{2,1},{3,2},{4,3},{5,4},{6,5},{7,6},{0,7},{9,8},{10,9},{11,1... | collective-permute-start | bytes 27656 | tf_op jit(solution)/shard_map/ppermute | solution.py:18
  117.3 4.4 %collective-permute-start.13 = (bf16[1,16,2,128]{3,2,1,0:T(2,128)(2,1)S(1)}, bf16[1,16,2,128]{3,2,1,0:T(2,128)(2,1)S(1)}, u32[]{:S(2)}, u32[]{:S(2)}) collective-permute-start(bf16[1,16,2,128]{3,2,1,0:T(2,128)(2,1)S(1)} %bitcast.376), channel_id=1, source_target_pairs={{8,0},{16,8},{24,16},{0,24},{9,1},{17,9},{25,17},{1,25},{10,2},{18... | collective-permute-start | bytes 24584 | tf_op jit(solution)/shard_map/ppermute | solution.py:18
  120.9 4.3 %collective-permute-start.12 = (bf16[1,16,2,128]{3,2,1,0:T(2,128)(2,1)S(1)}, bf16[1,16,2,128]{3,2,1,0:T(2,128)(2,1)S(1)}, u32[]{:S(2)}, u32[]{:S(2)}) collective-permute-start(bf16[1,16,2,128]{3,2,1,0:T(2,128)(2,1)S(1)} %bitcast.375), channel_id=1, source_target_pairs={{0,8},{8,16},{16,24},{24,0},{1,9},{9,17},{17,25},{25,1},{2,10},{10... | collective-permute-start | bytes 24584 | tf_op jit(solution)/shard_map/ppermute | solution.py:17
  125.2 2.3 %collective-permute-start.14 = (bf16[18,1,2,128]{3,2,1,0:T(2,128)(2,1)S(1)}, bf16[18,1,2,128]{3,2,1,0:T(2,128)(2,1)S(1)}, u32[]{:S(2)}, u32[]{:S(2)}) collective-permute-start(bf16[18,1,2,128]{3,2,1,0:T(2,128)(2,1)S(1)} %get-tuple-element.75), channel_id=1, source_target_pairs={{0,1},{1,2},{2,3},{3,4},{4,5},{5,6},{6,7},{7,0},{8,9},{9,10},{10,1... | collective-permute-start | bytes 27656 | tf_op jit(solution)/shard_map/ppermute | solution.py:17
  126.7 4.0 %collective-permute-start.15 = (bf16[18,1,2,128]{3,2,1,0:T(2,128)(2,1)S(1)}, bf16[18,1,2,128]{3,2,1,0:T(2,128)(2,1)S(1)}, u32[]{:S(2)}, u32[]{:S(2)}) collective-permute-start(bf16[18,1,2,128]{3,2,1,0:T(2,128)(2,1)S(1)} %get-tuple-element.76), channel_id=1, source_target_pairs={{1,0},{2,1},{3,2},{4,3},{5,4},{6,5},{7,6},{0,7},{9,8},{10,9},{11,1... | collective-permute-start | bytes 27656 | tf_op jit(solution)/shard_map/ppermute | solution.py:18
  134.0 4.6 %collective-permute-start.16 = (bf16[1,32,2,256]{3,2,1,0:T(2,128)(2,1)S(1)}, bf16[1,32,2,256]{3,2,1,0:T(2,128)(2,1)S(1)}, u32[]{:S(2)}, u32[]{:S(2)}) collective-permute-start(bf16[1,32,2,256]{3,2,1,0:T(2,128)(2,1)S(1)} %get-tuple-element.16), channel_id=1, source_target_pairs={{0,8},{8,16},{16,24},{24,0},{1,9},{9,17},{17,25},{25,1},{2,10},{10... | collective-permute-start | bytes 98312 | tf_op jit(solution)/shard_map/ppermute | solution.py:17
  134.1 4.6 %collective-permute-start.17 = (bf16[1,32,2,256]{3,2,1,0:T(2,128)(2,1)S(1)}, bf16[1,32,2,256]{3,2,1,0:T(2,128)(2,1)S(1)}, u32[]{:S(2)}, u32[]{:S(2)}) collective-permute-start(bf16[1,32,2,256]{3,2,1,0:T(2,128)(2,1)S(1)} %get-tuple-element.17), channel_id=1, source_target_pairs={{8,0},{16,8},{24,16},{0,24},{9,1},{17,9},{25,17},{1,25},{10,2},{18... | collective-permute-start | bytes 98312 | tf_op jit(solution)/shard_map/ppermute | solution.py:18
  138.7 2.3 %collective-permute-start.18 = (bf16[34,1,2,256]{3,2,1,0:T(2,128)(2,1)S(1)}, bf16[34,1,2,256]{3,2,1,0:T(2,128)(2,1)S(1)}, u32[]{:S(2)}, u32[]{:S(2)}) collective-permute-start(bf16[34,1,2,256]{3,2,1,0:T(2,128)(2,1)S(1)} %get-tuple-element.14), channel_id=1, source_target_pairs={{0,1},{1,2},{2,3},{3,4},{4,5},{5,6},{6,7},{7,0},{8,9},{9,10},{10,1... | collective-permute-start | bytes 104456 | tf_op jit(solution)/shard_map/ppermute | solution.py:17
  139.9 4.3 %collective-permute-start.19 = (bf16[34,1,2,256]{3,2,1,0:T(2,128)(2,1)S(1)}, bf16[34,1,2,256]{3,2,1,0:T(2,128)(2,1)S(1)}, u32[]{:S(2)}, u32[]{:S(2)}) collective-permute-start(bf16[34,1,2,256]{3,2,1,0:T(2,128)(2,1)S(1)} %get-tuple-element.15), channel_id=1, source_target_pairs={{1,0},{2,1},{3,2},{4,3},{5,4},{6,5},{7,6},{0,7},{9,8},{10,9},{11,1... | collective-permute-start | bytes 104456 | tf_op jit(solution)/shard_map/ppermute | solution.py:18
  184.0 4.5 %collective-permute-start.21 = (bf16[1,32,2,128]{3,2,1,0:T(2,128)(2,1)S(1)}, bf16[1,32,2,128]{3,2,1,0:T(2,128)(2,1)S(1)}, u32[]{:S(2)}, u32[]{:S(2)}) collective-permute-start(bf16[1,32,2,128]{3,2,1,0:T(2,128)(2,1)S(1)} %bitcast.374), channel_id=1, source_target_pairs={{8,0},{16,8},{24,16},{0,24},{9,1},{17,9},{25,17},{1,25},{10,2},{18... | collective-permute-start | bytes 49160 | tf_op jit(solution)/shard_map/ppermute | solution.py:18
  187.6 4.4 %collective-permute-start.20 = (bf16[1,32,2,128]{3,2,1,0:T(2,128)(2,1)S(1)}, bf16[1,32,2,128]{3,2,1,0:T(2,128)(2,1)S(1)}, u32[]{:S(2)}, u32[]{:S(2)}) collective-permute-start(bf16[1,32,2,128]{3,2,1,0:T(2,128)(2,1)S(1)} %bitcast.372), channel_id=1, source_target_pairs={{0,8},{8,16},{16,24},{24,0},{1,9},{9,17},{17,25},{25,1},{2,10},{10... | collective-permute-start | bytes 49160 | tf_op jit(solution)/shard_map/ppermute | solution.py:17
  192.1 2.4 %collective-permute-start.22 = (bf16[34,1,2,128]{3,2,1,0:T(2,128)(2,1)S(1)}, bf16[34,1,2,128]{3,2,1,0:T(2,128)(2,1)S(1)}, u32[]{:S(2)}, u32[]{:S(2)}) collective-permute-start(bf16[34,1,2,128]{3,2,1,0:T(2,128)(2,1)S(1)} %get-tuple-element.45), channel_id=1, source_target_pairs={{0,1},{1,2},{2,3},{3,4},{4,5},{5,6},{6,7},{7,0},{8,9},{9,10},{10,1... | collective-permute-start | bytes 52232 | tf_op jit(solution)/shard_map/ppermute | solution.py:17
  193.6 4.1 %collective-permute-start.23 = (bf16[34,1,2,128]{3,2,1,0:T(2,128)(2,1)S(1)}, bf16[34,1,2,128]{3,2,1,0:T(2,128)(2,1)S(1)}, u32[]{:S(2)}, u32[]{:S(2)}) collective-permute-start(bf16[34,1,2,128]{3,2,1,0:T(2,128)(2,1)S(1)} %get-tuple-element.46), channel_id=1, source_target_pairs={{1,0},{2,1},{3,2},{4,3},{5,4},{6,5},{7,6},{0,7},{9,8},{10,9},{11,1... | collective-permute-start | bytes 52232 | tf_op jit(solution)/shard_map/ppermute | solution.py:18
  (13 other events, 253.5 us)
Sparse Core Ops, SparseCore 0:
  9.2 29.5 all-gather.1
where the time goes:
time: 216 us
  local copies, waits for them, and re-layouts  71.4 us (33%)
  waiting for transfers between devices  68.8 us (32%)
  starting transfers between devices  30 us (14%)
  matrix products  16.6 us (8%)
  other arithmetic  14.8 us (7%)
  between operations  14.2 us (7%)
    slice x6, local copies, waits for them, and re-layouts, conv_valid(): padded[row_step:row_step + height, col_step:col_step + width]  27.9 us
    all_gather x1, waiting for transfers between devices, body(): lax.all_gather(source_tiles, 'col', axis=1, tiled=True).reshape(-1, columns)  27.5 us
    ppermute x12, waiting for transfers between devices, with_halo(): after = lax.ppermute(leading, axis, down)  21.7 us
    ppermute x12, starting transfers between devices, with_halo(): after = lax.ppermute(leading, axis, down)  18.9 us
    ppermute x12, waiting for transfers between devices, with_halo(): before = lax.ppermute(last, axis, up)  18.9 us
    dot_general x54, matrix products, conv_valid(): jnp.dot(window, weight[row_step, col_step], preferred_element_type=jnp.fl...  16.3 us
    reshape x9, local copies, waits for them, and re-layouts, conv_valid(): padded[row_step:row_step + height, col_step:col_step + width]  14.8 us
    gather x1, local copies, waits for them, and re-layouts, body(): picked = buffer[stencil]  12.1 us
  transfers between devices with their start and end apart: 25, of which 22 were waited for; matrix products, arithmetic and copies ran while one was open for 2% of the time, Pallas kernels for 0%

commit v1 on v0

--- a/solution.py
+++ b/solution.py
@@ -5,6 +5,23 @@
 
 FIELDS = 64
 CH = 128
+
+
+def arrange_row(mat, at_axis):
+    q_n = lax.axis_size("col")
+    in_order = [(nth, (nth + 1) % q_n) for nth in range(q_n)]
+    parts_seen = [(nth, (nth - 1) % q_n) for nth in range(q_n)]
+    v_next, item_now = ([mat], [mat])
+    for _ in range(q_n // 2):
+        val2 = lax.ppermute(v_next[-1], axis_name="col", perm=in_order)
+        v_next.append(val2)
+    for _ in [*range((q_n - 1) // 2)]:
+        vec_out = lax.ppermute(item_now[-1], axis_name="col", perm=parts_seen)
+        item_now.append(vec_out)
+    taken_in = jnp.concatenate([*v_next[::-1], *item_now[1:]], axis=at_axis)
+    inter = lax.axis_index("col")
+    extra = jnp.roll(taken_in, (inter - q_n // 2) * mat.shape[at_axis], axis=at_axis)
+    return extra
 
 
 def with_halo(x, sides, width):
@@ -69,7 +86,7 @@
     wanted = requests.reshape(groups, capacity)
     global_ids = (jnp.arange(groups, dtype=jnp.int32)[:, None] * cells + wanted).reshape(-1)
     empty = jnp.zeros((groups * capacity, columns), jnp.bfloat16)
-    flattened = lax.all_gather(source_tiles, "col", axis=1, tiled=True).reshape(-1, columns)
+    flattened = arrange_row(source_tiles, 1).reshape(-1, columns)
     inside = (global_ids >= 0) & (global_ids < flattened.shape[0])
     picked = flattened[jnp.clip(global_ids, 0, flattened.shape[0] - 1)]
     buffer = jnp.where(inside[:, None], picked, empty)

time: 216 us -> 192 us (0.89)
  waiting for transfers between devices: 68.8 us -> 46.7 us
  starting transfers between devices: 30 us -> 43.8 us
  between operations: 14.2 us -> 1 us
  local copies, waits for them, and re-layouts: 71.4 us -> 67.7 us
    all_gather x1 -> x0, waiting for transfers between devices: 27.5 us -> none  [body(): lax.all_gather(source_tiles, 'col', axis=1, tiled=True).reshape(-1, columns)]
    ppermute x0 -> x7, waiting for transfers between devices: none -> 18.7 us  [the longest x4 15.8 us: arrange_row(): val2 = lax.ppermute(v_next[-1], axis_name='col', perm=in_order)]
    ppermute x0 -> x7, starting transfers between devices: none -> 11.9 us  [the longest x4 11.8 us: arrange_row(): val2 = lax.ppermute(v_next[-1], axis_name='col', perm=in_order)]
    ppermute x12, waiting for transfers between devices: 18.9 us -> 10.6 us  [with_halo(): before = lax.ppermute(last, axis, up)]
    ppermute x12, waiting for transfers between devices: 21.7 us -> 17.4 us  [with_halo(): after = lax.ppermute(leading, axis, down)]
    ppermute x12, starting transfers between devices: 11.1 us -> 14.5 us  [with_halo(): before = lax.ppermute(last, axis, up)]
    unnamed x32 -> x47, local copies, waits for them, and re-layouts: 6.32 us -> 3.71 us
  transfers between devices with their start and end apart: 25 -> 31, of which waited for: 22 -> 22; matrix products, arithmetic and copies ran while one was open for 2% -> 3% of each run, Pallas kernels for 0% -> 0%
where the time goes in v1:
time: 192 us
  local copies, waits for them, and re-layouts  67.7 us (35%)
  waiting for transfers between devices  46.7 us (24%)
  starting transfers between devices  43.8 us (23%)
  matrix products  17.9 us (9%)
  other arithmetic  14.8 us (8%)
    slice x6, local copies, waits for them, and re-layouts, conv_valid(): padded[row_step:row_step + height, col_step:col_step + width]  27.9 us
    dot_general x54, matrix products, conv_valid(): jnp.dot(window, weight[row_step, col_step], preferred_element_type=jnp.fl...  17.6 us
    ppermute x12, waiting for transfers between devices, with_halo(): after = lax.ppermute(leading, axis, down)  17.4 us
    ppermute x12, starting transfers between devices, with_halo(): after = lax.ppermute(leading, axis, down)  17.4 us
    ppermute x4, waiting for transfers between devices, arrange_row(): val2 = lax.ppermute(v_next[-1], axis_name='col', perm=in_order)  15.8 us
    reshape x9, local copies, waits for them, and re-layouts, conv_valid(): padded[row_step:row_step + height, col_step:col_step + width]  14.8 us
    ppermute x12, starting transfers between devices, with_halo(): before = lax.ppermute(last, axis, up)  14.5 us
    gather x1, local copies, waits for them, and re-layouts, body(): picked = buffer[stencil]  12.1 us
  transfers between devices with their start and end apart: 31, of which 22 were waited for; matrix products, arithmetic and copies ran while one was open for 3% of the time, Pallas kernels for 0%

profile of v1, /device:TPU:3, one launch (start us, length us, event | category | flops | bytes accessed | tf_op | source)
XLA Modules:
  0.0 191.8 jit_solution(14603352234749171055)
XLA Ops:
  3.3 4.1 %collective-permute-done = bf16[1,1,1024,128]{3,2,1,0:T(8,128)(2,1)S(1)} collective-permute-done((bf16[1,1,1024,128]{3,2,1,0:T(8,128)(2,1)}, bf16[1,1,1024,128]{3,2,1,0:T(8,128)(2,1)S(1)}, u32[]{:S(2)}, u32[]{:S(2)}) %collective-permute-start) | collective-permute-done | bytes 262176 | tf_op jit(solution)/shard_map/ppermute | solution.py:16
  7.4 3.3 %collective-permute-start.1 = (bf16[1,1,1024,128]{3,2,1,0:T(8,128)(2,1)S(1)}, bf16[1,1,1024,128]{3,2,1,0:T(8,128)(2,1)S(1)}, u32[]{:S(2)}, u32[]{:S(2)}) collective-permute-start(bf16[1,1,1024,128]{3,2,1,0:T(8,128)(2,1)S(1)} %collective-permute-done), channel_id=1, source_target_pairs={{0,1},{1,2},{2,3},{3,4},{4,5},{5,6},{6,7},{7,0},{8,9},{9,10},{10,1... | collective-permute-start | bytes 786440 | tf_op jit(solution)/shard_map/ppermute | solution.py:16
  10.7 3.3 %collective-permute-done.1 = bf16[1,1,1024,128]{3,2,1,0:T(8,128)(2,1)S(1)} collective-permute-done((bf16[1,1,1024,128]{3,2,1,0:T(8,128)(2,1)S(1)}, bf16[1,1,1024,128]{3,2,1,0:T(8,128)(2,1)S(1)}, u32[]{:S(2)}, u32[]{:S(2)}) %collective-permute-start.1) | collective-permute-done | bytes 262176 | tf_op jit(solution)/shard_map/ppermute | solution.py:16
  14.0 3.4 %collective-permute-start.2 = (bf16[1,1,1024,128]{3,2,1,0:T(8,128)(2,1)S(1)}, bf16[1,1,1024,128]{3,2,1,0:T(8,128)(2,1)S(1)}, u32[]{:S(2)}, u32[]{:S(2)}) collective-permute-start(bf16[1,1,1024,128]{3,2,1,0:T(8,128)(2,1)S(1)} %collective-permute-done.1), channel_id=1, source_target_pairs={{0,1},{1,2},{2,3},{3,4},{4,5},{5,6},{6,7},{7,0},{8,9},{9,10},{10,1... | collective-permute-start | bytes 786440 | tf_op jit(solution)/shard_map/ppermute | solution.py:16
  18.3 4.9 %collective-permute-done.2 = bf16[1,1,1024,128]{3,2,1,0:T(8,128)(2,1)S(1)} collective-permute-done((bf16[1,1,1024,128]{3,2,1,0:T(8,128)(2,1)S(1)}, bf16[1,1,1024,128]{3,2,1,0:T(8,128)(2,1)S(1)}, u32[]{:S(2)}, u32[]{:S(2)}) %collective-permute-start.2) | collective-permute-done | bytes 262176 | tf_op jit(solution)/shard_map/ppermute | solution.py:16
  23.2 3.4 %collective-permute-start.3 = (bf16[1,1,1024,128]{3,2,1,0:T(8,128)(2,1)S(1)}, bf16[1,1,1024,128]{3,2,1,0:T(8,128)(2,1)S(1)}, u32[]{:S(2)}, u32[]{:S(2)}) collective-permute-start(bf16[1,1,1024,128]{3,2,1,0:T(8,128)(2,1)S(1)} %collective-permute-done.2), channel_id=1, source_target_pairs={{0,1},{1,2},{2,3},{3,4},{4,5},{5,6},{6,7},{7,0},{8,9},{9,10},{10,1... | collective-permute-start | bytes 786440 | tf_op jit(solution)/shard_map/ppermute | solution.py:16
  28.4 3.5 %collective-permute-done.3 = bf16[1,1,1024,128]{3,2,1,0:T(8,128)(2,1)S(1)} collective-permute-done((bf16[1,1,1024,128]{3,2,1,0:T(8,128)(2,1)S(1)}, bf16[1,1,1024,128]{3,2,1,0:T(8,128)(2,1)S(1)}, u32[]{:S(2)}, u32[]{:S(2)}) %collective-permute-start.3) | collective-permute-done | bytes 262176 | tf_op jit(solution)/shard_map/ppermute | solution.py:16
  32.2 2.9 %collective-permute-done.6 = bf16[1,1,1024,128]{3,2,1,0:T(8,128)(2,1)S(1)} collective-permute-done((bf16[1,1,1024,128]{3,2,1,0:T(8,128)(2,1)S(1)}, bf16[1,1,1024,128]{3,2,1,0:T(8,128)(2,1)S(1)}, u32[]{:S(2)}, u32[]{:S(2)}) %collective-permute-start.6) | collective-permute-done | bytes 262176 | tf_op jit(solution)/shard_map/ppermute | solution.py:19
  35.6 6.2 %gather_fusion = bf16[2048,128]{1,0:T(8,128)(2,1)S(1)} fusion(bf16[8192,128]{1,0:T(8,128)(2,1)S(1)} %bitcast.300, s32[2048]{0:T(1024)S(1)} %broadcast_clamp_fusion.1), kind=kCustom, calls=%fused_computation | custom fusion | bytes 1056768 | tf_op jit(solution)/shard_map/gather | solution.py:91
  42.1 12.1 %gather_fusion.1 = bf16[4096,128]{1,0:T(8,128)(2,1)S(1)} fusion(bf16[2048,128]{1,0:T(8,128)(2,1)S(1)} %broadcast_select_fusion.4, s32[4096]{0:T(1024)S(1)} %broadcast_clamp_fusion), kind=kCustom, calls=%fused_computation.1 | custom fusion | bytes 2113536 | tf_op jit(solution)/shard_map/gather | solution.py:93
  66.2 5.2 %fusion.120 = (bf16[32,32,2,64]{3,2,1,0:T(2,128)(2,1)S(1)}, bf16[32,32,2,64]{3,2,1,0:T(2,128)(2,1)S(1)}, bf16[32,32,2,64]{3,2,1,0:T(2,128)(2,1)S(1)}, bf16[32,32...) fusion(bf16[34,34,2,64]{3,2,1,0:T(2,128)(2,1)S(1)} %broadcast_s, ...), kind=kLoop, calls=%fused_computation.235 | loop fusion | bytes 4718592 | tf_op jit(solution)/shard_map/slice | solution.py:49
  74.2 3.3 %collective-permute-start.12 = (bf16[1,32,2,128]{3,2,1,0:T(2,128)(2,1)S(1)}, bf16[1,32,2,128]{3,2,1,0:T(2,128)(2,1)S(1)}, u32[]{:S(2)}, u32[]{:S(2)}) collective-permute-start(bf16[1,32,2,128]{3,2,1,0:T(2,128)(2,1)S(1)} %bitcast.369), channel_id=1, source_target_pairs={{8,0},{16,8},{24,16},{0,24},{9,1},{17,9},{25,17},{1,25},{10,2},{18... | collective-permute-start | bytes 49160 | tf_op jit(solution)/shard_map/ppermute | solution.py:35
  78.6 3.8 %collective-permute-start.13 = (bf16[34,1,2,128]{3,2,1,0:T(2,128)(2,1)S(1)}, bf16[34,1,2,128]{3,2,1,0:T(2,128)(2,1)S(1)}, u32[]{:S(2)}, u32[]{:S(2)}) collective-permute-start(bf16[34,1,2,128]{3,2,1,0:T(2,128)(2,1)S(1)} %get-tuple-element.47), channel_id=1, source_target_pairs={{0,1},{1,2},{2,3},{3,4},{4,5},{5,6},{6,7},{7,0},{8,9},{9,10},{10,1... | collective-permute-start | bytes 52232 | tf_op jit(solution)/shard_map/ppermute | solution.py:34
  83.3 3.2 %collective-permute-done.14 = bf16[34,1,2,128]{3,2,1,0:T(2,128)(2,1)S(1)} collective-permute-done((bf16[34,1,2,128]{3,2,1,0:T(2,128)(2,1)S(1)}, bf16[34,1,2,128]{3,2,1,0:T(2,128)(2,1)S(1)}, u32[]{:S(2)}, u32[]{:S(2)}) %collective-permute-start.14) | collective-permute-done | bytes 17440 | tf_op jit(solution)/shard_map/ppermute | solution.py:35
  88.3 5.2 %fusion.119 = (bf16[32,32,2,128]{3,2,1,0:T(2,128)(2,1)S(1)}, bf16[32,32,2,128]{3,2,1,0:T(2,128)(2,1)S(1)}, bf16[32,32,2,128]{3,2,1,0:T(2,128)(2,1)S(1)}, bf16[32...) fusion(bf16[34,34,2,128]{3,2,1,0:T(2,128)(2,1)S(1)} %broadcast_, ...), kind=kLoop, calls=%fused_computation.234 | loop fusion | bytes 9437184 | tf_op jit(solution)/shard_map/slice | solution.py:49
  97.5 3.2 %collective-permute-start.16 = (bf16[1,16,2,128]{3,2,1,0:T(2,128)(2,1)S(1)}, bf16[1,16,2,128]{3,2,1,0:T(2,128)(2,1)S(1)}, u32[]{:S(2)}, u32[]{:S(2)}) collective-permute-start(bf16[1,16,2,128]{3,2,1,0:T(2,128)(2,1)S(1)} %get-tuple-element.82), channel_id=1, source_target_pairs={{8,0},{16,8},{24,16},{0,24},{9,1},{17,9},{25,17},{1,25},{10,2},{18... | collective-permute-start | bytes 24584 | tf_op jit(solution)/shard_map/ppermute | solution.py:35
  103.4 3.2 %collective-permute-done.18 = bf16[18,1,2,128]{3,2,1,0:T(2,128)(2,1)S(1)} collective-permute-done((bf16[18,1,2,128]{3,2,1,0:T(2,128)(2,1)S(1)}, bf16[18,1,2,128]{3,2,1,0:T(2,128)(2,1)S(1)}, u32[]{:S(2)}, u32[]{:S(2)}) %collective-permute-start.18) | collective-permute-done | bytes 9248 | tf_op jit(solution)/shard_map/ppermute | solution.py:35
  110.2 2.8 %collective-permute-start.20 = (bf16[1,16,2,128]{3,2,1,0:T(2,128)(2,1)S(1)}, bf16[1,16,2,128]{3,2,1,0:T(2,128)(2,1)S(1)}, u32[]{:S(2)}, u32[]{:S(2)}) collective-permute-start(bf16[1,16,2,128]{3,2,1,0:T(2,128)(2,1)S(1)} %bitcast.373), channel_id=1, source_target_pairs={{8,0},{16,8},{24,16},{0,24},{9,1},{17,9},{25,17},{1,25},{10,2},{18... | collective-permute-start | bytes 24584 | tf_op jit(solution)/shard_map/ppermute | solution.py:35
  115.8 3.2 %collective-permute-done.22 = bf16[18,1,2,128]{3,2,1,0:T(2,128)(2,1)S(1)} collective-permute-done((bf16[18,1,2,128]{3,2,1,0:T(2,128)(2,1)S(1)}, bf16[18,1,2,128]{3,2,1,0:T(2,128)(2,1)S(1)}, u32[]{:S(2)}, u32[]{:S(2)}) %collective-permute-start.22) | collective-permute-done | bytes 9248 | tf_op jit(solution)/shard_map/ppermute | solution.py:35
  129.3 3.2 %collective-permute-done.26 = bf16[34,1,2,256]{3,2,1,0:T(2,128)(2,1)S(1)} collective-permute-done((bf16[34,1,2,256]{3,2,1,0:T(2,128)(2,1)S(1)}, bf16[34,1,2,256]{3,2,1,0:T(2,128)(2,1)S(1)}, u32[]{:S(2)}, u32[]{:S(2)}) %collective-permute-start.26) | collective-permute-done | bytes 34848 | tf_op jit(solution)/shard_map/ppermute | solution.py:35
  132.5 5.8 %broadcast_select_fusion = bf16[34,34,2,256]{3,2,1,0:T(2,128)(2,1)S(1)} fusion(pred[34]{0:T(512)(128)(4,1)S(1)} %compare_and_fusion.2, bf16[34,1,2,256]{3,2,1,0:T(2,128)(2,1)S(1)} %collective-permute-done.26, bf16[1,32,2,256]{3,2,1,0:T(2,128)(2,1)S(1)} %collective-permute-done.24, bf16[32,32,2,128]{3,2,1,0:T(2,128)(2,1)S(1)} %bitcast.304, ...), kind=kLoop, calls=%fused_computation.34 | loop fusion | flops 7694336 | bytes 2367522 | tf_op jit(solution)/shard_map/jit(_where)/select_n | solution.py:63
  138.3 10.7 %fusion.117 = (bf16[32,32,2,256]{3,2,1,0:T(2,128)(2,1)}, bf16[32,32,2,256]{3,2,1,0:T(2,128)(2,1)}, bf16[32,32,2,256]{3,2,1,0:T(2,128)(2,1)S(1)}, bf16[32,32,2,25...) fusion(bf16[34,34,2,256]{3,2,1,0:T(2,128)(2,1)S(1)} %broadcast_, ...), kind=kLoop, calls=%fused_computation.232 | loop fusion | bytes 18874368 | tf_op jit(solution)/shard_map/slice | solution.py:49
  177.3 3.2 %collective-permute-done.30 = bf16[34,1,2,128]{3,2,1,0:T(2,128)(2,1)S(1)} collective-permute-done((bf16[34,1,2,128]{3,2,1,0:T(2,128)(2,1)S(1)}, bf16[34,1,2,128]{3,2,1,0:T(2,128)(2,1)S(1)}, u32[]{:S(2)}, u32[]{:S(2)}) %collective-permute-start.30) | collective-permute-done | bytes 17440 | tf_op jit(solution)/shard_map/ppermute | solution.py:35
  182.2 5.2 %fusion.118 = (bf16[32,32,2,128]{3,2,1,0:T(2,128)(2,1)S(1)}, bf16[32,32,2,128]{3,2,1,0:T(2,128)(2,1)S(1)}, bf16[32,32,2,128]{3,2,1,0:T(2,128)(2,1)S(1)}, bf16[32...) fusion(bf16[34,34,2,128]{3,2,1,0:T(2,128)(2,1)S(1)} %broadcast_, ...), kind=kLoop, calls=%fused_computation.233 | loop fusion | bytes 9437184 | tf_op jit(solution)/shard_map/slice | solution.py:49
  (198 shorter events, 82.5 us)
Async XLA Ops:
  0.0 7.4 %collective-permute-start = (bf16[1,1,1024,128]{3,2,1,0:T(8,128)(2,1)}, bf16[1,1,1024,128]{3,2,1,0:T(8,128)(2,1)S(1)}, u32[]{:S(2)}, u32[]{:S(2)}) collective-permute-start(bf16[1,1,1024,128]{3,2,1,0:T(8,128)(2,1)} %param.11), channel_id=1, source_target_pairs={{0,1},{1,2},{2,3},{3,4},{4,5},{5,6},{6,7},{7,0},{8,9},{9,10},{10,1... | collective-permute-start | bytes 786440 | tf_op jit(solution)/shard_map/ppermute | solution.py:16
  1.8 16.5 %collective-permute-start.4 = (bf16[1,1,1024,128]{3,2,1,0:T(8,128)(2,1)}, bf16[1,1,1024,128]{3,2,1,0:T(8,128)(2,1)S(1)}, u32[]{:S(2)}, u32[]{:S(2)}) collective-permute-start(bf16[1,1,1024,128]{3,2,1,0:T(8,128)(2,1)} %param.11), channel_id=1, source_target_pairs={{0,7},{1,0},{2,1},{3,2},{4,3},{5,4},{6,5},{7,6},{8,15},{9,8},{10,9... | collective-permute-start | bytes 786440 | tf_op jit(solution)/shard_map/ppermute | solution.py:19
  7.4 6.6 %collective-permute-start.1 = (bf16[1,1,1024,128]{3,2,1,0:T(8,128)(2,1)S(1)}, bf16[1,1,1024,128]{3,2,1,0:T(8,128)(2,1)S(1)}, u32[]{:S(2)}, u32[]{:S(2)}) collective-permute-start(bf16[1,1,1024,128]{3,2,1,0:T(8,128)(2,1)S(1)} %collective-permute-done), channel_id=1, source_target_pairs={{0,1},{1,2},{2,3},{3,4},{4,5},{5,6},{6,7},{7,0},{8,9},{9,10},{10,1... | collective-permute-start | bytes 786440 | tf_op jit(solution)/shard_map/ppermute | solution.py:16
  14.0 9.2 %collective-permute-start.2 = (bf16[1,1,1024,128]{3,2,1,0:T(8,128)(2,1)S(1)}, bf16[1,1,1024,128]{3,2,1,0:T(8,128)(2,1)S(1)}, u32[]{:S(2)}, u32[]{:S(2)}) collective-permute-start(bf16[1,1,1024,128]{3,2,1,0:T(8,128)(2,1)S(1)} %collective-permute-done.1), channel_id=1, source_target_pairs={{0,1},{1,2},{2,3},{3,4},{4,5},{5,6},{6,7},{7,0},{8,9},{9,10},{10,1... | collective-permute-start | bytes 786440 | tf_op jit(solution)/shard_map/ppermute | solution.py:16
  18.3 10.0 %collective-permute-start.5 = (bf16[1,1,1024,128]{3,2,1,0:T(8,128)(2,1)S(1)}, bf16[1,1,1024,128]{3,2,1,0:T(8,128)(2,1)S(1)}, u32[]{:S(2)}, u32[]{:S(2)}) collective-permute-start(bf16[1,1,1024,128]{3,2,1,0:T(8,128)(2,1)S(1)} %collective-permute-done.4), channel_id=1, source_target_pairs={{0,7},{1,0},{2,1},{3,2},{4,3},{5,4},{6,5},{7,6},{8,15},{9,8},{10,9... | collective-permute-start | bytes 786440 | tf_op jit(solution)/shard_map/ppermute | solution.py:19
  23.2 8.6 %collective-permute-start.3 = (bf16[1,1,1024,128]{3,2,1,0:T(8,128)(2,1)S(1)}, bf16[1,1,1024,128]{3,2,1,0:T(8,128)(2,1)S(1)}, u32[]{:S(2)}, u32[]{:S(2)}) collective-permute-start(bf16[1,1,1024,128]{3,2,1,0:T(8,128)(2,1)S(1)} %collective-permute-done.2), channel_id=1, source_target_pairs={{0,1},{1,2},{2,3},{3,4},{4,5},{5,6},{6,7},{7,0},{8,9},{9,10},{10,1... | collective-permute-start | bytes 786440 | tf_op jit(solution)/shard_map/ppermute | solution.py:16
  28.3 6.7 %collective-permute-start.6 = (bf16[1,1,1024,128]{3,2,1,0:T(8,128)(2,1)S(1)}, bf16[1,1,1024,128]{3,2,1,0:T(8,128)(2,1)S(1)}, u32[]{:S(2)}, u32[]{:S(2)}) collective-permute-start(bf16[1,1,1024,128]{3,2,1,0:T(8,128)(2,1)S(1)} %collective-permute-done.5), channel_id=1, source_target_pairs={{0,7},{1,0},{2,1},{3,2},{4,3},{5,4},{6,5},{7,6},{8,15},{9,8},{10,9... | collective-permute-start | bytes 786440 | tf_op jit(solution)/shard_map/ppermute | solution.py:19
  56.0 4.4 %collective-permute-start.7 = (bf16[1,32,2,64]{3,2,1,0:T(2,128)(2,1)S(1)}, bf16[1,32,2,64]{3,2,1,0:T(2,128)(2,1)S(1)}, u32[]{:S(2)}, u32[]{:S(2)}) collective-permute-start(bf16[1,32,2,64]{3,2,1,0:T(2,128)(2,1)S(1)} %slice.421), channel_id=1, source_target_pairs={{0,8},{8,16},{16,24},{24,0},{1,9},{9,17},{17,25},{25,1},{2,10},{10... | collective-permute-start | bytes 24584 | tf_op jit(solution)/shard_map/ppermute | solution.py:34
  56.8 4.1 %collective-permute-start.8 = (bf16[1,32,2,64]{3,2,1,0:T(2,128)(2,1)S(1)}, bf16[1,32,2,64]{3,2,1,0:T(2,128)(2,1)S(1)}, u32[]{:S(2)}, u32[]{:S(2)}) collective-permute-start(bf16[1,32,2,64]{3,2,1,0:T(2,128)(2,1)S(1)} %slice.423), channel_id=1, source_target_pairs={{8,0},{16,8},{24,16},{0,24},{9,1},{17,9},{25,17},{1,25},{10,2},{18... | collective-permute-start | bytes 24584 | tf_op jit(solution)/shard_map/ppermute | solution.py:35
  61.0 4.1 %collective-permute-start.10 = (bf16[34,1,2,64]{3,2,1,0:T(2,128)(2,1)S(1)}, bf16[34,1,2,64]{3,2,1,0:T(2,128)(2,1)S(1)}, u32[]{:S(2)}, u32[]{:S(2)}) collective-permute-start(bf16[34,1,2,64]{3,2,1,0:T(2,128)(2,1)S(1)} %get-tuple-element.50), channel_id=1, source_target_pairs={{1,0},{2,1},{3,2},{4,3},{5,4},{6,5},{7,6},{0,7},{9,8},{10,9},{11,1... | collective-permute-start | bytes 26120 | tf_op jit(solution)/shard_map/ppermute | solution.py:35
  61.0 4.1 %collective-permute-start.9 = (bf16[34,1,2,64]{3,2,1,0:T(2,128)(2,1)S(1)}, bf16[34,1,2,64]{3,2,1,0:T(2,128)(2,1)S(1)}, u32[]{:S(2)}, u32[]{:S(2)}) collective-permute-start(bf16[34,1,2,64]{3,2,1,0:T(2,128)(2,1)S(1)} %get-tuple-element.49), channel_id=1, source_target_pairs={{0,1},{1,2},{2,3},{3,4},{4,5},{5,6},{6,7},{7,0},{8,9},{9,10},{10,1... | collective-permute-start | bytes 26120 | tf_op jit(solution)/shard_map/ppermute | solution.py:34
  74.1 4.4 %collective-permute-start.11 = (bf16[1,32,2,128]{3,2,1,0:T(2,128)(2,1)S(1)}, bf16[1,32,2,128]{3,2,1,0:T(2,128)(2,1)S(1)}, u32[]{:S(2)}, u32[]{:S(2)}) collective-permute-start(bf16[1,32,2,128]{3,2,1,0:T(2,128)(2,1)S(1)} %bitcast.371), channel_id=1, source_target_pairs={{0,8},{8,16},{16,24},{24,0},{1,9},{9,17},{17,25},{25,1},{2,10},{10... | collective-permute-start | bytes 49160 | tf_op jit(solution)/shard_map/ppermute | solution.py:34
  74.2 4.4 %collective-permute-start.12 = (bf16[1,32,2,128]{3,2,1,0:T(2,128)(2,1)S(1)}, bf16[1,32,2,128]{3,2,1,0:T(2,128)(2,1)S(1)}, u32[]{:S(2)}, u32[]{:S(2)}) collective-permute-start(bf16[1,32,2,128]{3,2,1,0:T(2,128)(2,1)S(1)} %bitcast.369), channel_id=1, source_target_pairs={{8,0},{16,8},{24,16},{0,24},{9,1},{17,9},{25,17},{1,25},{10,2},{18... | collective-permute-start | bytes 49160 | tf_op jit(solution)/shard_map/ppermute | solution.py:35
  78.6 4.7 %collective-permute-start.13 = (bf16[34,1,2,128]{3,2,1,0:T(2,128)(2,1)S(1)}, bf16[34,1,2,128]{3,2,1,0:T(2,128)(2,1)S(1)}, u32[]{:S(2)}, u32[]{:S(2)}) collective-permute-start(bf16[34,1,2,128]{3,2,1,0:T(2,128)(2,1)S(1)} %get-tuple-element.47), channel_id=1, source_target_pairs={{0,1},{1,2},{2,3},{3,4},{4,5},{5,6},{6,7},{7,0},{8,9},{9,10},{10,1... | collective-permute-start | bytes 52232 | tf_op jit(solution)/shard_map/ppermute | solution.py:34
  82.5 4.1 %collective-permute-start.14 = (bf16[34,1,2,128]{3,2,1,0:T(2,128)(2,1)S(1)}, bf16[34,1,2,128]{3,2,1,0:T(2,128)(2,1)S(1)}, u32[]{:S(2)}, u32[]{:S(2)}) collective-permute-start(bf16[34,1,2,128]{3,2,1,0:T(2,128)(2,1)S(1)} %get-tuple-element.48), channel_id=1, source_target_pairs={{1,0},{2,1},{3,2},{4,3},{5,4},{6,5},{7,6},{0,7},{9,8},{10,9},{11,1... | collective-permute-start | bytes 52232 | tf_op jit(solution)/shard_map/ppermute | solution.py:35
  97.0 4.6 %collective-permute-start.15 = (bf16[1,16,2,128]{3,2,1,0:T(2,128)(2,1)S(1)}, bf16[1,16,2,128]{3,2,1,0:T(2,128)(2,1)S(1)}, u32[]{:S(2)}, u32[]{:S(2)}) collective-permute-start(bf16[1,16,2,128]{3,2,1,0:T(2,128)(2,1)S(1)} %get-tuple-element.81), channel_id=1, source_target_pairs={{0,8},{8,16},{16,24},{24,0},{1,9},{9,17},{17,25},{25,1},{2,10},{10... | collective-permute-start | bytes 24584 | tf_op jit(solution)/shard_map/ppermute | solution.py:34
  97.5 4.1 %collective-permute-start.16 = (bf16[1,16,2,128]{3,2,1,0:T(2,128)(2,1)S(1)}, bf16[1,16,2,128]{3,2,1,0:T(2,128)(2,1)S(1)}, u32[]{:S(2)}, u32[]{:S(2)}) collective-permute-start(bf16[1,16,2,128]{3,2,1,0:T(2,128)(2,1)S(1)} %get-tuple-element.82), channel_id=1, source_target_pairs={{8,0},{16,8},{24,16},{0,24},{9,1},{17,9},{25,17},{1,25},{10,2},{18... | collective-permute-start | bytes 24584 | tf_op jit(solution)/shard_map/ppermute | solution.py:35
  102.6 4.0 %collective-permute-start.18 = (bf16[18,1,2,128]{3,2,1,0:T(2,128)(2,1)S(1)}, bf16[18,1,2,128]{3,2,1,0:T(2,128)(2,1)S(1)}, u32[]{:S(2)}, u32[]{:S(2)}) collective-permute-start(bf16[18,1,2,128]{3,2,1,0:T(2,128)(2,1)S(1)} %get-tuple-element.78), channel_id=1, source_target_pairs={{1,0},{2,1},{3,2},{4,3},{5,4},{6,5},{7,6},{0,7},{9,8},{10,9},{11,1... | collective-permute-start | bytes 27656 | tf_op jit(solution)/shard_map/ppermute | solution.py:35
  109.3 4.7 %collective-permute-start.19 = (bf16[1,16,2,128]{3,2,1,0:T(2,128)(2,1)S(1)}, bf16[1,16,2,128]{3,2,1,0:T(2,128)(2,1)S(1)}, u32[]{:S(2)}, u32[]{:S(2)}) collective-permute-start(bf16[1,16,2,128]{3,2,1,0:T(2,128)(2,1)S(1)} %bitcast.374), channel_id=1, source_target_pairs={{0,8},{8,16},{16,24},{24,0},{1,9},{9,17},{17,25},{25,1},{2,10},{10... | collective-permute-start | bytes 24584 | tf_op jit(solution)/shard_map/ppermute | solution.py:34
  115.0 4.0 %collective-permute-start.22 = (bf16[18,1,2,128]{3,2,1,0:T(2,128)(2,1)S(1)}, bf16[18,1,2,128]{3,2,1,0:T(2,128)(2,1)S(1)}, u32[]{:S(2)}, u32[]{:S(2)}) collective-permute-start(bf16[18,1,2,128]{3,2,1,0:T(2,128)(2,1)S(1)} %get-tuple-element.76), channel_id=1, source_target_pairs={{1,0},{2,1},{3,2},{4,3},{5,4},{6,5},{7,6},{0,7},{9,8},{10,9},{11,1... | collective-permute-start | bytes 27656 | tf_op jit(solution)/shard_map/ppermute | solution.py:35
  122.2 5.0 %collective-permute-start.23 = (bf16[1,32,2,256]{3,2,1,0:T(2,128)(2,1)S(1)}, bf16[1,32,2,256]{3,2,1,0:T(2,128)(2,1)S(1)}, u32[]{:S(2)}, u32[]{:S(2)}) collective-permute-start(bf16[1,32,2,256]{3,2,1,0:T(2,128)(2,1)S(1)} %get-tuple-element.16), channel_id=1, source_target_pairs={{0,8},{8,16},{16,24},{24,0},{1,9},{9,17},{17,25},{25,1},{2,10},{10... | collective-permute-start | bytes 98312 | tf_op jit(solution)/shard_map/ppermute | solution.py:34
  128.2 4.3 %collective-permute-start.26 = (bf16[34,1,2,256]{3,2,1,0:T(2,128)(2,1)S(1)}, bf16[34,1,2,256]{3,2,1,0:T(2,128)(2,1)S(1)}, u32[]{:S(2)}, u32[]{:S(2)}) collective-permute-start(bf16[34,1,2,256]{3,2,1,0:T(2,128)(2,1)S(1)} %get-tuple-element.15), channel_id=1, source_target_pairs={{1,0},{2,1},{3,2},{4,3},{5,4},{6,5},{7,6},{0,7},{9,8},{10,9},{11,1... | collective-permute-start | bytes 104456 | tf_op jit(solution)/shard_map/ppermute | solution.py:35
  170.5 4.8 %collective-permute-start.27 = (bf16[1,32,2,128]{3,2,1,0:T(2,128)(2,1)S(1)}, bf16[1,32,2,128]{3,2,1,0:T(2,128)(2,1)S(1)}, u32[]{:S(2)}, u32[]{:S(2)}) collective-permute-start(bf16[1,32,2,128]{3,2,1,0:T(2,128)(2,1)S(1)} %bitcast.372), channel_id=1, source_target_pairs={{0,8},{8,16},{16,24},{24,0},{1,9},{9,17},{17,25},{25,1},{2,10},{10... | collective-permute-start | bytes 49160 | tf_op jit(solution)/shard_map/ppermute | solution.py:34
  176.4 4.1 %collective-permute-start.30 = (bf16[34,1,2,128]{3,2,1,0:T(2,128)(2,1)S(1)}, bf16[34,1,2,128]{3,2,1,0:T(2,128)(2,1)S(1)}, u32[]{:S(2)}, u32[]{:S(2)}) collective-permute-start(bf16[34,1,2,128]{3,2,1,0:T(2,128)(2,1)S(1)} %get-tuple-element.46), channel_id=1, source_target_pairs={{1,0},{2,1},{3,2},{4,3},{5,4},{6,5},{7,6},{0,7},{9,8},{10,9},{11,1... | collective-permute-start | bytes 52232 | tf_op jit(solution)/shard_map/ppermute | solution.py:35
  (19 other events, 295.9 us)
